TPU v7x, 256 devices: a whole 4x4x8 slice. The times are simulated.
256 devices in a mesh: gy: 8 (over z), gx: 32 (over x, y, core).
Axes of the slice: x: 4, y: 4, z: 8, core: 2. Of those that a mesh axis runs over, the one named last changes fastest.
Arguments:
- depth_start: float32 [4, 1024, 4096], P(None, 'gy', 'gx'), may hold values from 0.3 to 0.5
- bed_height: float32 [1024, 4096], P('gy', 'gx'), may hold values from 0 to 4.2
- zone_map: int32 [1024, 4096], P('gy', 'gx'), may hold values from 0 to 15, as said below
- manning: float32 [16], replicated, may hold values from 0.04 to 0.3
- observe: float32 [4, 1024, 4096], P(None, 'gy', 'gx'), may hold values from -90 to 90
Outputs:
- final_depth: float32 [4, 1024, 4096], P(None, 'gy', 'gx')
- grad_start: float32 [4, 1024, 4096], P(None, 'gy', 'gx')
- zone_grad: float32 [16], replicated
Inputs may be any that keep to these rules, and one draw needn't show every extreme that they name: `zone_map`: constant on aligned patches of 8 x 8 cells.
All inputs are finite; a program needn't handle non-finite values.
Results may differ from a plain program's by a relative error of at most 0.0003.
Values sent between devices are 32-bit elements; how exact they have to be, the bound alone decides.
A program may use at most 64 MiB of HBM per device.

v0:
```python
import functools

import jax
import jax.numpy as jnp
from jax import lax
from jax.experimental import pallas as pl
from jax.experimental.pallas import tpu as pltpu
from jax.sharding import PartitionSpec as P

STEPS = 4
ZONES = 16
EVENTS = 4
GRAVITY = 9.81
TIME_STEP = 0.3
SPACING = 2.0
CENTRE = 0.7
FLOOR = 0.01

RATE = TIME_STEP / SPACING
ALPHA = RATE * GRAVITY * TIME_STEP / (2.0 * SPACING)
BETA = RATE * ALPHA
SIDE = 0.5 * (1.0 - CENTRE)
POWER = -7.0 / 3.0
FLOOR_SQ = (BETA * FLOOR) ** 2
ROUGH_SCALE = GRAVITY * TIME_STEP * (2.0 * ALPHA) ** (-POWER) / BETA
WALL = 1e20

ROWS = 128
LANES = 128
RIM = 8
EXT = ROWS + 2 * RIM
PAD = 8
TALL = EXT + 2 * PAD
BASE = PAD
WIDE = EVENTS + 1

MESH = pl.DeviceIdType.MESH


def lanes_of(shape):
    return lax.broadcasted_iota(jnp.int32, shape, len(shape) - 1)


def rows_of(shape):
    return lax.broadcasted_iota(jnp.int32, shape, len(shape) - 2)


def roll(value, shift, axis=None):
    axis = value.ndim - 1 if axis is None else axis
    return pltpu.roll(value, shift % value.shape[axis], axis)


def mesh_place():
    gy, gx = lax.axis_index("gy"), lax.axis_index("gx")
    ny, nx = lax.axis_size("gy"), lax.axis_size("gx")
    return gy, gx, ny, nx


def fill_own(manning, depth, bed, zone, observe, ext, msg_left, msg_right):
    own = pl.ds(RIM, ROWS)
    classes = zone[pl.ds(0, ROWS // 8, stride=8), :]
    rough = jnp.zeros(classes.shape, jnp.float32)
    for k in range(ZONES):
        m = manning[k]
        rough = jnp.where(classes == k, m * m * ROUGH_SCALE, rough)
    for i in range(ROWS // 8):
        ext[9, RIM + 8 * i : RIM + 8 * i + 8, :] = jnp.broadcast_to(rough[i : i + 1], (8, LANES))
    for e in range(EVENTS):
        ext[e, own, :] = depth[e] * ALPHA
        ext[EVENTS + e, own, :] = observe[e]
    ext[8, own, :] = bed[...] * ALPHA
    lane = lanes_of((ROWS, LANES))
    slot8 = lane // 8
    left = jnp.zeros((ROWS, LANES), jnp.float32)
    right = jnp.zeros((ROWS, LANES), jnp.float32)
    for q in range(10):
        value = ext[q, own, :]
        right = jnp.where(slot8 == q, roll(value, 8 * q + 8), right)
        for e in range(EVENTS):
            if q < EVENTS and q == e:
                at = 4 * e + 3
            elif EVENTS <= q < 8 and q == EVENTS + e:
                at = 4 * e + 2
            elif q == 8:
                at = 4 * e + 1
            elif q == 9:
                at = 4 * e
            else:
                continue
            left = jnp.where(slot8 == at, roll(value, 8 * at), left)
    msg_left[...] = left
    msg_right[...] = right


def neighbours():
    gy, gx, ny, nx = mesh_place()
    up, down = lax.rem(gy + ny - 1, ny), lax.rem(gy + 1, ny)
    west, east = lax.rem(gx + nx - 1, nx), lax.rem(gx + 1, nx)
    return gy, gx, up, down, west, east


def rim_copies(ext, col_left, col_right, msg_left, msg_right, send, recv):
    gy, gx, up, down, west, east = neighbours()
    plans = [
        (msg_left, col_right.at[pl.ds(RIM, ROWS)], (gy, west)),
        (msg_right, col_left.at[pl.ds(RIM, ROWS)], (gy, east)),
        (ext.at[:, pl.ds(ROWS, RIM)], ext.at[:, pl.ds(0, RIM)], (down, gx)),
        (ext.at[:, pl.ds(RIM, RIM)], ext.at[:, pl.ds(RIM + ROWS, RIM)], (up, gx)),
        (msg_left.at[pl.ds(ROWS - RIM, RIM)], col_right.at[pl.ds(0, RIM)], (down, west)),
        (msg_left.at[pl.ds(0, RIM)], col_right.at[pl.ds(RIM + ROWS, RIM)], (up, west)),
        (msg_right.at[pl.ds(ROWS - RIM, RIM)], col_left.at[pl.ds(0, RIM)], (down, east)),
        (msg_right.at[pl.ds(0, RIM)], col_left.at[pl.ds(RIM + ROWS, RIM)], (up, east)),
    ]
    return [
        pltpu.make_async_remote_copy(
            src_ref=src,
            dst_ref=dst,
            send_sem=send.at[i],
            recv_sem=recv.at[i],
            device_id=to,
            device_id_type=MESH,
        )
        for i, (src, dst, to) in enumerate(plans)
    ]


def greet_neighbours(barrier):
    gy, gx, up, down, west, east = neighbours()
    for to in [
        (gy, west),
        (gy, east),
        (down, gx),
        (up, gx),
        (down, west),
        (up, west),
        (down, east),
        (up, east),
    ]:
        pl.semaphore_signal(barrier, inc=1, device_id=to, device_id_type=MESH)


def exchange_kernel(
    manning, depth, bed, zone, observe, ext, col_left, col_right, msg_left, msg_right, send, recv
):
    barrier = pltpu.get_barrier_semaphore()
    greet_neighbours(barrier)
    fill_own(manning, depth, bed, zone, observe, ext, msg_left, msg_right)
    pl.semaphore_wait(barrier, 8)
    copies = rim_copies(ext, col_left, col_right, msg_left, msg_right, send, recv)
    for copy in copies:
        copy.start()
    for copy in copies:
        copy.wait()


def window_main(own, left, at):
    lane = lanes_of(own.shape)
    return jnp.where(lane < RIM, roll(left, -8 * at), roll(own, RIM))


def window_side(owns, right, at):
    lane = lanes_of(owns[0].shape)
    rolled = {}
    out = roll(right, 24 - 8 * at)
    for e, own in enumerate(owns):
        hit = (lane >= 32 * e) & (lane < 32 * e + 24)
        out = jnp.where(hit, roll(own, 24 + 32 * e), out)
    return out


def build_windows(ext, col_left, col_right, depth, bar, gbx, gby, rough_x, rough_y, ground):
    gy, gx, ny, nx = mesh_place()
    here = pl.ds(BASE, EXT)
    left, right = col_left[...], col_right[...]
    for e in range(EVENTS):
        depth[e, here, :] = window_main(ext[e], left, e)
        bar[e, here, :] = window_main(ext[EVENTS + e], left, EVENTS + e)
    depth[EVENTS, here, :] = window_side([ext[e] for e in range(EVENTS)], right, 3)
    bar[EVENTS, here, :] = window_side([ext[EVENTS + e] for e in range(EVENTS)], right, 2)
    shape = (EXT, LANES)
    lane = lanes_of(shape)
    row = rows_of(shape) + (gy * ROWS - RIM)
    wall_y = (row < 0) | (row >= ny * ROWS - 1)
    for w in range(2):
        if w == 0:
            high = window_main(ext[8], left, 8)
            rough = window_main(ext[9], left, 9)
            column = lane + (gx * LANES - RIM)
        else:
            high = window_side([ext[8]] * EVENTS, right, 1)
            rough = window_side([ext[9]] * EVENTS, right, 0)
            column = lane % 32 + (gx * LANES + 104)
        ground[w, here, :] = high
        gbx[w, here, :] = roll(high, -1) - high
        wall_x = (column < 0) | (column >= nx * LANES - 1)
        rough_x[w, here, :] = jnp.where(wall_x, WALL, rough)
        rough_y[w, here, :] = jnp.where(wall_y, WALL, rough)
    for w in range(2):
        gby[w, here, :] = ground[w, pl.ds(BASE + 1, EXT), :] - ground[w, here, :]


def inverse(x):
    y = pl.reciprocal(x, approx=True)
    return y * (2.0 - x * y)


def power_of(double_depth):
    return jnp.exp2((POWER / 0.6931471805599453) * jnp.log(double_depth))


def face(depth, depth_next, gap, flux, sides, rough, first):
    double = depth + depth_next
    slope = (depth_next - depth) + gap
    drive = double * slope
    p = power_of(double)
    if first:
        drag = rough * p * (BETA * FLOOR)
        push = -drive
    else:
        size = flux * flux + FLOOR_SQ
        drag = rough * p * (size * lax.rsqrt(size))
        push = CENTRE * flux + SIDE * sides - drive
    keep = inverse(1.0 + drag)
    return push * keep, drag, keep


def forward_chunk(t, r0, n, depth, fx, fy, drag_x, drag_y, keep_x, keep_y, gbx, gby, rough_x, rough_y):
    here, above, below = pl.ds(r0, n), pl.ds(r0 - 1, n), pl.ds(r0 + 1, n)
    first = t == 0
    for k in range(WIDE):
        w = k // EVENTS
        d = depth[t, k, here, :]
        if first:
            qx = qy = sx = sy = None
        else:
            qx = fx[t - 1, k, here, :]
            qy = fy[t - 1, k, here, :]
            sx = roll(qx, 1) + roll(qx, -1)
            sy = fy[t - 1, k, above, :] + fy[t - 1, k, below, :]
        nx, wx, kx = face(d, roll(d, -1), gbx[w, here, :], qx, sx, rough_x[w, here, :], first)
        ny, wy, ky = face(d, depth[t, k, below, :], gby[w, here, :], qy, sy, rough_y[w, here, :], first)
        fx[t, k, here, :] = nx
        fy[t, k, here, :] = ny
        drag_x[t, k, here, :] = wx
        drag_y[t, k, here, :] = wy
        keep_x[t, k, here, :] = kx
        keep_y[t, k, here, :] = ky
        depth[t + 1, k, here, :] = d + (roll(nx, 1) - nx) + (fy[t, k, above, :] - ny)


def face_back(bar_new, keep, new, drag, depth, depth_next, gap, flux, first):
    a = bar_new * keep
    term = a * (new * drag)
    both = (-POWER) * term * pl.reciprocal(depth + depth_next, approx=True)
    to_here = both + a * (depth + depth - gap)
    to_next = both - a * (depth_next + depth_next + gap)
    if first:
        return a, term, to_here, to_next, None
    size = flux * flux + FLOOR_SQ
    own = CENTRE * a - term * (flux * pl.reciprocal(size, approx=True))
    return a, term, to_here, to_next, own


def backward_chunk(
    t, r0, n, bar, depth, fx, fy, drag_x, drag_y, keep_x, keep_y, gbx, gby, bar_x, bar_y, side_y, down_y, classes
):
    here, above, below = pl.ds(r0, n), pl.ds(r0 - 1, n), pl.ds(r0 + 1, n)
    first = t == 0
    now, past = t % 2, (t + 1) % 2
    sums = [None, None]
    for k in range(WIDE):
        w = k // EVENTS
        bar_d = bar[past, k, here, :]
        back_x = roll(bar_d, -1) - bar_d
        back_y = bar[past, k, below, :] - bar_d
        if t < STEPS - 1:
            back_x = back_x + bar_x[past, k, here, :]
            back_y = back_y + (
                bar_y[past, k, here, :] + SIDE * (side_y[past, k, above, :] + side_y[past, k, below, :])
            )
        d = depth[t, k, here, :]
        qx = None if first else fx[t - 1, k, here, :]
        qy = None if first else fy[t - 1, k, here, :]
        ax, tx, hx, ex, ox = face_back(
            back_x, keep_x[t, k, here, :], fx[t, k, here, :], drag_x[t, k, here, :], d, roll(d, -1), gbx[w, here, :], qx, first
        )
        ay, ty, hy, ey, oy = face_back(
            back_y, keep_y[t, k, here, :], fy[t, k, here, :], drag_y[t, k, here, :], d, depth[t, k, below, :], gby[w, here, :], qy, first
        )
        sums[w] = tx + ty if sums[w] is None else sums[w] + (tx + ty)
        down_y[k, here, :] = ey
        bar[now, k, here, :] = bar_d + (hx + roll(ex, 1)) + (hy + down_y[k, above, :])
        if not first:
            bar_x[now, k, here, :] = ox + SIDE * (roll(ax, 1) + roll(ax, -1))
            bar_y[now, k, here, :] = oy
            side_y[now, k, here, :] = ay
    for w in range(2):
        if t == STEPS - 1:
            classes[w, here, :] = sums[w]
        else:
            classes[w, here, :] = classes[w, here, :] + sums[w]


def unwindow(mains, side, e):
    lane = lanes_of(mains.shape)
    return jnp.where(lane < 112, roll(mains, -RIM), roll(side, 104 - 32 * e))


def class_rows(manning, zone, classes, out):
    own = pl.ds(BASE + RIM, ROWS)
    main, side = classes[0, own, :], classes[1, own, :]
    lane = lanes_of(main.shape)
    tail = roll(side, 104)
    for e in range(1, EVENTS):
        tail = tail + roll(side, 104 - 32 * e)
    both = jnp.where(lane < 112, roll(main, -RIM), tail)
    kinds = zone[pl.ds(0, ROWS // 8, stride=8), :]
    rows = jnp.concatenate([jnp.sum(both[8 * i : 8 * i + 8], axis=0, keepdims=True) for i in range(ROWS // 8)], axis=0)
    lane8 = lanes_of((8, LANES))
    total = jnp.zeros((8, LANES), jnp.float32)
    for k in range(ZONES):
        part = jnp.where(kinds == k, rows, 0.0)
        s = jnp.sum(part)
        m = manning[k]
        total = jnp.where(lane8 == k, s, total)
    out[...] = total


def steps(kernel_rows, loop):
    for r0 in range(BASE, BASE + EXT, kernel_rows):
        loop(r0, min(kernel_rows, BASE + EXT - r0))


CHUNK = 24


def evolve_kernel(
    manning, zone, ext, col_left, col_right, final, grad, partial,
    depth, bar, gbx, gby, rough_x, rough_y, ground,
    fx, fy, drag_x, drag_y, keep_x, keep_y, bar_x, bar_y, side_y, down_y, classes,
):
    build_windows(ext, col_left, col_right, depth.at[0], bar.at[0], gbx, gby, rough_x, rough_y, ground)
    for t in range(STEPS):
        steps(CHUNK, lambda r0, n: forward_chunk(
            t, r0, n, depth, fx, fy, drag_x, drag_y, keep_x, keep_y, gbx, gby, rough_x, rough_y))
    own = pl.ds(BASE + RIM, ROWS)
    side = depth[STEPS, EVENTS, own, :]
    for e in range(EVENTS):
        final[e] = unwindow(depth[STEPS, e, own, :], side, e) * (1.0 / ALPHA)
    for t in reversed(range(STEPS)):
        steps(CHUNK, lambda r0, n: backward_chunk(
            t, r0, n, bar, depth, fx, fy, drag_x, drag_y, keep_x, keep_y, gbx, gby, bar_x, bar_y, side_y, down_y, classes))
    side = bar[0, EVENTS, own, :]
    for e in range(EVENTS):
        grad[e] = unwindow(bar[0, e, own, :], side, e)
    class_rows(manning, zone, classes, partial)


def sum_kernel(partial, total, slots_y, slots_x, send, recv):
    gy, gx, ny, nx = mesh_place()
    barrier = pltpu.get_barrier_semaphore()
    for off in range(1, ny):
        pl.semaphore_signal(barrier, inc=1, device_id=(lax.rem(gy + off, ny), gx), device_id_type=MESH)
    for off in range(1, nx):
        pl.semaphore_signal(barrier, inc=1, device_id=(gy, lax.rem(gx + off, nx)), device_id_type=MESH)
    pl.semaphore_wait(barrier, ny + nx - 2)
    value = partial[...]
    for stage, (slots, count, me) in enumerate([(slots_y, ny, gy), (slots_x, nx, gx)]):
        slots[me] = value
        copies = []
        for off in range(1, count):
            to = lax.rem(me + off, count)
            copies.append(
                pltpu.make_async_remote_copy(
                    src_ref=slots.at[me],
                    dst_ref=slots.at[me],
                    send_sem=send.at[stage],
                    recv_sem=recv.at[stage],
                    device_id=(to, gx) if stage == 0 else (gy, to),
                    device_id_type=MESH,
                )
            )
        for copy in copies:
            copy.start()
        everything = slots.at[pl.ds(0, count - 1)]
        pltpu.make_async_copy(everything, everything, recv.at[stage]).wait()
        value = slots[0]
        for i in range(1, count):
            value = value + slots[i]
        pltpu.make_async_copy(everything, everything, send.at[stage]).wait()
    total[...] = value


def vmem():
    return pl.BlockSpec(memory_space=pltpu.VMEM)


def smem():
    return pl.BlockSpec(memory_space=pltpu.SMEM)


def f32(*shape):
    return jax.ShapeDtypeStruct(shape, jnp.float32)


LIMIT = 60 * 1024 * 1024


def evolve_scratch():
    big = pltpu.VMEM((STEPS, WIDE, TALL, LANES), jnp.float32)
    pair = pltpu.VMEM((2, WIDE, TALL, LANES), jnp.float32)
    wide = pltpu.VMEM((2, TALL, LANES), jnp.float32)
    return [
        pltpu.VMEM((STEPS + 1, WIDE, TALL, LANES), jnp.float32),
        pair,
        wide, wide, wide, wide, wide,
        big, big, big, big, big, big,
        pair, pair, pair,
        pltpu.VMEM((WIDE, TALL, LANES), jnp.float32),
        wide,
    ]


def body(depth_start, bed_height, zone_map, manning, observe):
    ny, nx = lax.axis_size("gy"), lax.axis_size("gx")
    ext, col_left, col_right = pl.pallas_call(
        exchange_kernel,
        out_shape=(f32(10, EXT, LANES), f32(EXT, LANES), f32(EXT, LANES)),
        in_specs=[smem(), vmem(), vmem(), vmem(), vmem()],
        out_specs=(vmem(), vmem(), vmem()),
        scratch_shapes=[
            pltpu.VMEM((ROWS, LANES), jnp.float32),
            pltpu.VMEM((ROWS, LANES), jnp.float32),
            pltpu.SemaphoreType.DMA((8,)),
            pltpu.SemaphoreType.DMA((8,)),
        ],
        compiler_params=pltpu.CompilerParams(collective_id=0, has_side_effects=True),
        name="exchange",
    )(manning, depth_start, bed_height, zone_map, observe)
    final, grad, partial = pl.pallas_call(
        evolve_kernel,
        out_shape=(f32(EVENTS, ROWS, LANES), f32(EVENTS, ROWS, LANES), f32(8, LANES)),
        in_specs=[smem(), vmem(), vmem(), vmem(), vmem()],
        out_specs=(vmem(), vmem(), vmem()),
        scratch_shapes=evolve_scratch(),
        compiler_params=pltpu.CompilerParams(vmem_limit_bytes=LIMIT),
        name="evolve",
    )(manning, zone_map, ext, col_left, col_right)
    total = pl.pallas_call(
        sum_kernel,
        out_shape=f32(8, LANES),
        in_specs=[vmem()],
        out_specs=vmem(),
        scratch_shapes=[
            pltpu.VMEM((ny, 8, LANES), jnp.float32),
            pltpu.VMEM((nx, 8, LANES), jnp.float32),
            pltpu.SemaphoreType.DMA((2,)),
            pltpu.SemaphoreType.DMA((2,)),
        ],
        compiler_params=pltpu.CompilerParams(collective_id=1, has_side_effects=True),
        name="sum_classes",
    )(partial)
    zone_grad = total[0, :ZONES] * (-2.0 / ALPHA) / manning
    return final, grad, zone_grad


def solution(mesh):
    in_specs = (P(None, "gy", "gx"), P("gy", "gx"), P("gy", "gx"), P(), P(None, "gy", "gx"))
    out_specs = (P(None, "gy", "gx"), P(None, "gy", "gx"), P())
    return jax.shard_map(body, mesh=mesh, in_specs=in_specs, out_specs=out_specs, check_vma=False)
```

profile of v0, /device:TPU:1, one launch (start us, length us, event | category | flops | bytes accessed | tf_op | source)
XLA Modules:
  0.0 59.8 jit_solution(5421819058834750248)
XLA Ops:
  0.6 16.5 %exchange.1 = (f32[10,144,128]{2,1,0:T(8,128)}, f32[144,128]{1,0:T(8,128)}, f32[144,128]{1,0:T(8,128)}) custom-call(f32[16]{0:T(128)} %manning.3, f32[4,128,128]{2,1,0:T(8,128)} %depth.1, f32[128,128]{1,0:T(8,128)} %bed.1, s32[128,128]{1,0:T(8,128)} %zone.3, f32[4,128,128]{2,1,0:T(8,128)} %observe.1), custom_call_target="tpu_custom_call" | custom-call | tf_op jit(solution)/shard_map/exchange/pallas_call | solution.py:426
  17.1 26.2 %evolve.1 = (f32[4,128,128]{2,1,0:T(8,128)}, f32[4,128,128]{2,1,0:T(8,128)}, f32[8,128]{1,0:T(8,128)}) custom-call(f32[16]{0:T(128)} %manning.3, s32[128,128]{1,0:T(8,128)} %zone.3, f32[10,144,128]{2,1,0:T(8,128)} %get-tuple-element.9.ext, f32[144,128]{1,0:T(8,128)} %get-tuple-element.10.col_left, f32[144,128]{1,0:T(8,128)} %get-tuple-element.11.col_right), custom_call_target="tpu_custom_call" | custom-call | tf_op jit(solution)/shard_map/evolve/pallas_call | solution.py:440
  43.3 0.0 copy-start
  43.3 15.3 %sum_classes.1 = f32[8,128]{1,0:T(8,128)} custom-call(f32[8,128]{1,0:T(8,128)} %get-tuple-element.14.partial), custom_call_target="tpu_custom_call" | custom-call | tf_op jit(solution)/shard_map/sum_classes/pallas_call | solution.py:449
  58.6 0.0 copy-done
  58.6 1.2 %bitcast_divide_fusion = f32[16]{0:T(128)} fusion(f32[16]{0:T(128)S(1)} %copy-done, f32[8,128]{1,0:T(8,128)} %sum_classes.1), kind=kLoop, calls=%fused_computation | loop fusion | flops 32 | bytes 192 | tf_op jit(solution)/shard_map/div | solution.py:463
Async XLA Ops:
  43.3 15.3 %copy-start = (f32[16]{0:T(128)S(1)}, f32[16]{0:T(128)}, u32[]{:S(2)}) copy-start(f32[16]{0:T(128)} %manning.3) | copy-start | bytes 196
where the time goes:
time: 60 us; the launch traced here: 59.8 us
  Pallas kernels  57.9 us (96%)
  other arithmetic  1.2 us (2%)
  between operations  0.66 us (1%)
    pallas_call x1, Pallas kernels, body(): pl.pallas_call(evolve_kernel, out_shape=(f32(EVENTS, ROWS, LANES), f32(EV...  26.2 us
    pallas_call x1, Pallas kernels, body(): pl.pallas_call(exchange_kernel, out_shape=(f32(10, EXT, LANES), f32(EXT,...  16.5 us
    pallas_call x1, Pallas kernels, body(): pl.pallas_call(sum_kernel, out_shape=f32(8, LANES), in_specs=[vmem()], ou...  15.3 us

commit v1 on v0

v1 whole, which is shorter than its diff:
```python
import collections
import functools

import jax
import jax.numpy as jnp
from jax import lax
from jax.experimental import pallas as pl
from jax.experimental.pallas import tpu as pltpu
from jax.sharding import PartitionSpec as P

STEPS = 4
ZONES = 16
EVENTS = 4
GRAVITY = 9.81
TIME_STEP = 0.3
SPACING = 2.0
CENTRE = 0.7
FLOOR = 0.01

RATE = TIME_STEP / SPACING
SIDE = 0.5 * (1.0 - CENTRE)
MID = CENTRE / SIDE
ALPHA = RATE * GRAVITY * TIME_STEP / (2.0 * SPACING * SIDE)
BETA = RATE * ALPHA
POWER = -7.0 / 3.0
FLOOR_SQ = (BETA * FLOOR) ** 2
ROUGH_SCALE = GRAVITY * TIME_STEP * (2.0 * ALPHA) ** (-POWER) / (BETA * SIDE)
WALL = 1e20

ROWS = 128
LANES = 128
RIM = 8
EXT = ROWS + 2 * RIM
PAD = 8
TALL = EXT + 2 * PAD
BASE = PAD
WIDE = EVENTS + 1

MESH = pl.DeviceIdType.MESH


def lanes_of(shape):
    return lax.broadcasted_iota(jnp.int32, shape, len(shape) - 1)


def rows_of(shape):
    return lax.broadcasted_iota(jnp.int32, shape, len(shape) - 2)


def roll(value, shift, axis=None):
    axis = value.ndim - 1 if axis is None else axis
    return pltpu.roll(value, shift % value.shape[axis], axis)


def mesh_place():
    gy, gx = lax.axis_index("gy"), lax.axis_index("gx")
    ny, nx = lax.axis_size("gy"), lax.axis_size("gx")
    return gy, gx, ny, nx


def own_copies(depth, bed, zone, observe, ext, zone_here, sems):
    own = pl.ds(RIM, ROWS)
    pairs = [
        (zone, zone_here),
        (bed, ext.at[8, own]),
        (depth, ext.at[pl.ds(0, EVENTS), own]),
        (observe, ext.at[pl.ds(EVENTS, EVENTS), own]),
    ]
    return [pltpu.make_async_copy(src, dst, sems.at[i]) for i, (src, dst) in enumerate(pairs)]


def fill_rough(manning, zone, ext):
    classes = zone[pl.ds(0, ROWS // 8, stride=8), :]
    rough = jnp.zeros(classes.shape, jnp.float32)
    for k in range(ZONES):
        m = manning[k]
        rough = jnp.where(classes == k, m * m * ROUGH_SCALE, rough)
    for i in range(ROWS // 8):
        ext[9, RIM + 8 * i : RIM + 8 * i + 8, :] = jnp.broadcast_to(rough[i : i + 1], (8, LANES))


def pack_rims(ext, msg_left, msg_right):
    def one(i, carry):
        here, own = pl.ds(pl.multiple_of(32 * i, 8), 32), pl.ds(pl.multiple_of(32 * i + RIM, 8), 32)
        slot8 = lanes_of((32, LANES)) // 8
        left = jnp.zeros((32, LANES), jnp.float32)
        right = jnp.zeros((32, LANES), jnp.float32)
        for q in range(10):
            value = ext[q, own, :]
            right = jnp.where(slot8 == q, roll(value, 8 * q + 8), right)
            for e in range(EVENTS):
                at = {e: 4 * e + 3, EVENTS + e: 4 * e + 2, 8: 4 * e + 1, 9: 4 * e}.get(q)
                if at is not None:
                    left = jnp.where(slot8 == at, roll(value, 8 * at), left)
        msg_left[here, :] = left
        msg_right[here, :] = right
        return carry

    lax.fori_loop(0, ROWS // 32, one, 0)


def neighbours():
    gy, gx, ny, nx = mesh_place()
    up, down = lax.rem(gy + ny - 1, ny), lax.rem(gy + 1, ny)
    west, east = lax.rem(gx + nx - 1, nx), lax.rem(gx + 1, nx)
    return gy, gx, up, down, west, east


def rim_copies(ext, col_left, col_right, msg_left, msg_right, send, recv):
    gy, gx, up, down, west, east = neighbours()
    plans = [
        (msg_left, col_right.at[pl.ds(RIM, ROWS)], (gy, west)),
        (msg_right, col_left.at[pl.ds(RIM, ROWS)], (gy, east)),
        (ext.at[:, pl.ds(ROWS, RIM)], ext.at[:, pl.ds(0, RIM)], (down, gx)),
        (ext.at[:, pl.ds(RIM, RIM)], ext.at[:, pl.ds(RIM + ROWS, RIM)], (up, gx)),
        (msg_left.at[pl.ds(ROWS - RIM, RIM)], col_right.at[pl.ds(0, RIM)], (down, west)),
        (msg_left.at[pl.ds(0, RIM)], col_right.at[pl.ds(RIM + ROWS, RIM)], (up, west)),
        (msg_right.at[pl.ds(ROWS - RIM, RIM)], col_left.at[pl.ds(0, RIM)], (down, east)),
        (msg_right.at[pl.ds(0, RIM)], col_left.at[pl.ds(RIM + ROWS, RIM)], (up, east)),
    ]
    return [
        pltpu.make_async_remote_copy(
            src_ref=src,
            dst_ref=dst,
            send_sem=send.at[i],
            recv_sem=recv.at[i],
            device_id=to,
            device_id_type=MESH,
        )
        for i, (src, dst, to) in enumerate(plans)
    ]


def greet_neighbours(barrier):
    gy, gx, up, down, west, east = neighbours()
    for to in [
        (gy, west),
        (gy, east),
        (down, gx),
        (up, gx),
        (down, west),
        (up, west),
        (down, east),
        (up, east),
    ]:
        pl.semaphore_signal(barrier, inc=1, device_id=to, device_id_type=MESH)


def window_main(own, left, at):
    lane = lanes_of(own.shape)
    return jnp.where(lane < RIM, roll(left, -8 * at), roll(own, RIM))


def window_side(owns, right, at):
    lane = lanes_of(owns[0].shape)
    rolled = {}
    out = roll(right, 24 - 8 * at)
    for e, own in enumerate(owns):
        hit = (lane >= 32 * e) & (lane < 32 * e + 24)
        out = jnp.where(hit, roll(own, 24 + 32 * e), out)
    return out


def windows_chunk(r0, n, ext, col_left, col_right, depth, bar, gbx, gby, rough_x, rough_y, ground):
    gy, gx, ny, nx = mesh_place()
    here, at = pl.ds(r0, n), pl.ds(r0 - BASE, n)
    left, right = col_left[at, :], col_right[at, :]
    value = [ext[q, at, :] for q in range(10)]
    for e in range(EVENTS):
        depth[e, here, :] = window_main(value[e], left, e) * ALPHA
        bar[e, here, :] = window_main(value[EVENTS + e], left, EVENTS + e)
    depth[EVENTS, here, :] = window_side(value[:EVENTS], right, 3) * ALPHA
    bar[EVENTS, here, :] = window_side(value[EVENTS:8], right, 2)
    shape = (n, LANES)
    lane = lanes_of(shape)
    row = rows_of(shape) + (gy * ROWS - RIM - BASE + r0)
    wall_y = (row < 0) | (row >= ny * ROWS - 1)
    for w in range(2):
        if w == 0:
            high = window_main(value[8], left, 8)
            rough = window_main(value[9], left, 9)
            column = lane + (gx * LANES - RIM)
        else:
            high = window_side([value[8]] * EVENTS, right, 1)
            rough = window_side([value[9]] * EVENTS, right, 0)
            column = lane % 32 + (gx * LANES + 104)
        high = high * ALPHA
        ground[w, here, :] = high
        gbx[w, here, :] = roll(high, -1) - high
        gby[w, pl.ds(r0 - 8, n), :] = ground[w, pl.ds(r0 - 7, n), :] - ground[w, pl.ds(r0 - 8, n), :]
        wall_x = (column < 0) | (column >= nx * LANES - 1)
        rough_x[w, here, :] = jnp.where(wall_x, WALL, rough)
        rough_y[w, here, :] = jnp.where(wall_y, WALL, rough)


def inverse(x):
    return pl.reciprocal(x, approx=True)


def face(depth, depth_next, gap, flux, sides, rough, first):
    double = depth + depth_next
    slope = (depth_next - depth) + gap
    drive = double * slope
    drag = rough * jnp.exp2((POWER / 0.6931471805599453) * jnp.log(double))
    if first:
        drag = drag * (BETA * FLOOR)
        keep = inverse(drag + 1.0 / SIDE)
        new = keep * (-drive)
    else:
        size = flux * flux + FLOOR_SQ
        turn = lax.rsqrt(size)
        drag = drag * (size * turn)
        keep = inverse(drag + 1.0 / SIDE)
        new = keep * ((MID * flux + sides) - drive)
    term = new * drag
    both = ((-POWER) * term) * inverse(double) - slope
    own = None if first else MID - term * ((flux * turn) * turn)
    return new, keep, term, both + double, both - double, own


def forward_chunk(first, last, t, r0, n, v):
    here, above, below = pl.ds(r0, n), pl.ds(r0 - 1, n), pl.ds(r0 + 1, n)
    for k in range(WIDE):
        w = k // EVENTS
        d = v.depth[t, k, here, :]
        if first:
            qx = qy = sx = sy = None
        else:
            qx = v.fx[t - 1, k, here, :]
            qy = v.fy[t - 1, k, here, :]
            sx = roll(qx, 1) + roll(qx, -1)
            sy = v.fy[t - 1, k, above, :] + v.fy[t - 1, k, below, :]
        nx, kx, zx, hx, ex, ox = face(d, roll(d, -1), v.gbx[w, here, :], qx, sx, v.rough_x[w, here, :], first)
        ny, ky, zy, hy, ey, oy = face(d, v.depth[t, k, below, :], v.gby[w, here, :], qy, sy, v.rough_y[w, here, :], first)
        v.fx[t, k, here, :] = nx
        v.fy[t, k, here, :] = ny
        v.keep_x[t, k, here, :] = kx
        v.keep_y[t, k, here, :] = ky
        v.term_x[t, k, here, :] = zx
        v.term_y[t, k, here, :] = zy
        v.here_x[t, k, here, :] = hx
        v.here_y[t, k, here, :] = hy
        v.next_x[t, k, here, :] = ex
        v.next_y[t, k, here, :] = ey
        if not first:
            v.own_x[t, k, here, :] = ox
            v.own_y[t, k, here, :] = oy
        v.depth[t + 1, k, here, :] = d + (roll(nx, 1) - nx) + (v.fy[t, k, above, :] - ny)


def backward_chunk(first, last, t, r0, n, v):
    here, above, below = pl.ds(r0, n), pl.ds(r0 - 1, n), pl.ds(r0 + 1, n)
    sums = [None, None]
    for k in range(WIDE):
        w = k // EVENTS
        bar_d = v.bar[t + 1, k, here, :]
        back_x = roll(bar_d, -1) - bar_d
        back_y = v.bar[t + 1, k, below, :] - bar_d
        if not last:
            back_x = back_x + v.bar_x[t + 1, k, here, :]
            back_y = back_y + (
                v.bar_y[t + 1, k, here, :] + (v.side_y[t + 1, k, above, :] + v.side_y[t + 1, k, below, :])
            )
        ax = back_x * v.keep_x[t, k, here, :]
        ay = back_y * v.keep_y[t, k, here, :]
        both = ax * v.term_x[t, k, here, :] + ay * v.term_y[t, k, here, :]
        sums[w] = both if sums[w] is None else sums[w] + both
        v.side_y[t, k, here, :] = ay
        if first:
            v.side_x[k, here, :] = ax
            continue
        v.down_y[k, here, :] = ay * v.next_y[t, k, here, :]
        v.bar[t, k, here, :] = (
            bar_d
            + (ax * v.here_x[t, k, here, :] + roll(ax * v.next_x[t, k, here, :], 1))
            + (ay * v.here_y[t, k, here, :] + v.down_y[k, above, :])
        )
        v.bar_x[t, k, here, :] = ax * v.own_x[t, k, here, :] + (roll(ax, 1) + roll(ax, -1))
        v.bar_y[t, k, here, :] = ay * v.own_y[t, k, here, :]
    for w in range(2):
        if last:
            v.classes[w, here, :] = sums[w]
        else:
            v.classes[w, here, :] = v.classes[w, here, :] + sums[w]


def start_chunk(r0, n, v):
    here, above = pl.ds(r0, n), pl.ds(r0 - 1, n)
    for k in range(WIDE):
        ax, ay = v.side_x[k, here, :], v.side_y[0, k, here, :]
        v.down_y[k, here, :] = ay * v.next_y[0, k, here, :]
        v.bar[0, k, here, :] = (
            v.bar[1, k, here, :]
            + (ax * v.here_x[0, k, here, :] + roll(ax * v.next_x[0, k, here, :], 1))
            + (ay * v.here_y[0, k, here, :] + v.down_y[k, above, :])
        )


def unwindow(window, side, e):
    return jnp.where(lanes_of(side.shape) < 112, roll(window, -RIM), roll(side, 104 - 32 * e))


def class_row(manning, zone, classes):
    own = pl.ds(BASE + RIM, ROWS)
    main, side = classes[0, own, :], classes[1, own, :]
    lane = lanes_of(main.shape)
    tail = roll(side, 104)
    for e in range(1, EVENTS):
        tail = tail + roll(side, 104 - 32 * e)
    both = jnp.where(lane < 112, roll(main, -RIM), tail)
    kinds = zone[pl.ds(0, ROWS // 8, stride=8), :]
    rows = jnp.concatenate([jnp.sum(both[8 * i : 8 * i + 8], axis=0, keepdims=True) for i in range(ROWS // 8)], axis=0)
    parts = [jnp.sum(jnp.where(kinds == k, rows, 0.0), axis=0, keepdims=True) for k in range(ZONES)]
    sums = jnp.sum(jnp.concatenate(parts, axis=0), axis=1, keepdims=True)
    square = (ZONES, LANES)
    row = jnp.sum(jnp.where(rows_of(square) == lanes_of(square), sums, 0.0), axis=0, keepdims=True)
    lane1 = lanes_of(row.shape)
    each = jnp.ones(row.shape, jnp.float32)
    for k in range(ZONES):
        each = jnp.where(lane1 == k, manning[k], each)
    return row * (-2.0 / ALPHA) / each


SUB = 24


def chunks(rows, step, sub=None):
    sub = min(sub or rows, rows)

    def one(i, carry):
        for j in range(0, rows, sub):
            step(pl.multiple_of(BASE + i * rows + j, 8), sub)
        return carry

    lax.fori_loop(0, EXT // rows, one, 0)


CHUNK_F = 72
CHUNK_B = 72
CHUNK_W = 48
CHUNK_A = 72


FULL = ("fx", "fy", "keep_x", "keep_y", "term_x", "term_y", "here_x", "here_y", "next_x", "next_y", "own_x", "own_y")
FULL += ("bar_x", "bar_y", "side_y")
PLANE = ("ground", "gbx", "gby", "rough_x", "rough_y", "classes")
NAMES = FULL + PLANE + ("depth", "bar", "side_x", "down_y")
Views = collections.namedtuple("Views", NAMES)


def view_scratch():
    tall = (TALL, LANES)
    shapes = [(STEPS, WIDE) + tall] * len(FULL) + [(2,) + tall] * len(PLANE)
    shapes += [(STEPS + 1, WIDE) + tall] * 2 + [(WIDE,) + tall] * 2
    return [pltpu.VMEM(shape, jnp.float32) for shape in shapes]


def over_steps(low, high, down, run):
    if not LOOP_T:
        for t in reversed(range(low, high)) if down else range(low, high):
            run(t)
        return

    def one(i, carry):
        run(high - 1 - i if down else low + i)
        return carry

    lax.fori_loop(0, high - low, one, 0)


LOOP_T = False


def forward(v, ext, col_left, col_right):
    chunks(CHUNK_W, lambda r0, n: windows_chunk(
        r0, n, ext, col_left, col_right, v.depth.at[0], v.bar.at[STEPS], v.gbx, v.gby, v.rough_x, v.rough_y, v.ground))
    last = pl.ds(BASE + EXT - 8, 8)
    for w in range(2):
        v.gby[w, last, :] = v.ground[w, pl.ds(BASE + EXT - 7, 8), :] - v.ground[w, last, :]
    chunks(CHUNK_F, lambda r0, n: forward_chunk(True, False, 0, r0, n, v))
    over_steps(1, STEPS, False, lambda t: chunks(CHUNK_F, lambda r0, n: forward_chunk(False, False, t, r0, n, v)))


def backward(v):
    chunks(CHUNK_B, lambda r0, n: backward_chunk(False, True, STEPS - 1, r0, n, v))
    over_steps(1, STEPS - 1, True, lambda t: chunks(CHUNK_B, lambda r0, n: backward_chunk(False, False, t, r0, n, v)))
    chunks(CHUNK_A, lambda r0, n: backward_chunk(True, False, 0, r0, n, v))


def stage_of(which):
    gy, gx, ny, nx = mesh_place()
    return (ny, gy) if which == 0 else (nx, gx)


def stage_peers(which):
    gy, gx, ny, nx = mesh_place()
    if which == 0:
        far = sorted(range(1, ny), key=lambda off: -min(off, ny - off))
        return [(lax.rem(gy + off, ny), gx) for off in far]
    if nx % 32:
        return [(gy, lax.rem(gx + off, nx)) for off in range(1, nx)]
    x, y, core = gx // 8, lax.rem(gx // 2, 4), lax.rem(gx, 2)
    xs = [lax.rem(x + d, nx // 8) * 8 for d in range(nx // 8)]
    ys = [lax.rem(y + d, 4) * 2 for d in range(4)]
    cores = [core, 1 - core]
    hops = lambda d, n: min(d, n - d)
    steps = [(dx, dy, dc) for dx in range(nx // 8) for dy in range(4) for dc in range(2)][1:]
    steps.sort(key=lambda d: -(2 * hops(d[0], nx // 8) + 2 * hops(d[1], 4) + d[2]))
    return [(gy, xs[dx] + ys[dy] + cores[dc]) for dx, dy, dc in steps]


def greet_stage(barrier, which):
    for to in stage_peers(which):
        pl.semaphore_signal(barrier, inc=1, device_id=to, device_id_type=MESH)


def send_stage(which, value, slots, send, recv):
    count, me = stage_of(which)
    slots[me] = value
    for to in stage_peers(which):
        pltpu.make_async_remote_copy(
            src_ref=slots.at[me],
            dst_ref=slots.at[me],
            send_sem=send.at[which],
            recv_sem=recv.at[which],
            device_id=to,
            device_id_type=MESH,
        ).start()


def sum_stage(which, slots, recv):
    count, me = stage_of(which)
    others = slots.at[pl.ds(0, count - 1)]
    pltpu.make_async_copy(others, others, recv.at[which]).wait()
    return jnp.sum(slots[...], axis=0)


def drain_stage(which, slots, send):
    count, me = stage_of(which)
    others = slots.at[pl.ds(0, count - 1)]
    pltpu.make_async_copy(others, others, send.at[which]).wait()


def kernel(
    manning, depth, bed, zone, observe, final, grad, total,
    ext, zone_here, col_left, col_right, msg_left, msg_right, slots_y, slots_x,
    own_sems, rim_send, rim_recv, sum_send, sum_recv, out_sems, *views,
):
    v = Views(*views)
    gy, gx, ny, nx = mesh_place()
    barrier = pltpu.get_barrier_semaphore()
    copies = own_copies(depth, bed, zone, observe, ext, zone_here, own_sems)
    for copy in copies:
        copy.start()
    greet_neighbours(barrier)
    greet_stage(barrier, 0)
    greet_stage(barrier, 1)
    for copy in copies:
        copy.wait()
    fill_rough(manning, zone_here, ext)
    pack_rims(ext, msg_left, msg_right)
    pl.semaphore_wait(barrier, 8 + ny - 1 + nx - 1)
    rims = rim_copies(ext, col_left, col_right, msg_left, msg_right, rim_send, rim_recv)
    for copy in rims:
        copy.start()
    for copy in rims:
        copy.wait()
    forward(v, ext, col_left, col_right)
    own = pl.ds(BASE + RIM, ROWS)
    final_copy = pltpu.make_async_copy(v.depth.at[STEPS, :, own], final, out_sems.at[0])
    final_copy.start()
    backward(v)
    send_stage(0, class_row(manning, zone_here, v.classes), slots_y, sum_send, sum_recv)
    chunks(CHUNK_A, lambda r0, n: start_chunk(r0, n, v))
    grad_copy = pltpu.make_async_copy(v.bar.at[0, :, own], grad, out_sems.at[1])
    grad_copy.start()
    send_stage(1, sum_stage(0, slots_y, sum_recv), slots_x, sum_send, sum_recv)
    final_copy.wait()
    drain_stage(0, slots_y, sum_send)
    total[...] = sum_stage(1, slots_x, sum_recv)
    drain_stage(1, slots_x, sum_send)
    grad_copy.wait()


def vmem():
    return pl.BlockSpec(memory_space=pltpu.VMEM)


def smem():
    return pl.BlockSpec(memory_space=pltpu.SMEM)


def f32(*shape):
    return jax.ShapeDtypeStruct(shape, jnp.float32)


LIMIT = 60 * 1024 * 1024


def finish_kernel(final_windows, grad_windows, total, final, grad, zone_grad):
    final_side, grad_side = final_windows[EVENTS], grad_windows[EVENTS]
    for e in range(EVENTS):
        final[e] = unwindow(final_windows[e], final_side, e) * (1.0 / ALPHA)
        grad[e] = unwindow(grad_windows[e], grad_side, e)
    zone_grad[...] = total[0, :ZONES]


def anywhere():
    return pl.BlockSpec(memory_space=pl.ANY)


def body(depth_start, bed_height, zone_map, manning, observe):
    ny, nx = lax.axis_size("gy"), lax.axis_size("gx")
    block = pltpu.VMEM((ROWS, LANES), jnp.float32)
    rim = pltpu.VMEM((EXT, LANES), jnp.float32)
    final_windows, grad_windows, total = pl.pallas_call(
        kernel,
        out_shape=(f32(WIDE, ROWS, LANES), f32(WIDE, ROWS, LANES), f32(1, LANES)),
        in_specs=[smem(), anywhere(), anywhere(), anywhere(), anywhere()],
        out_specs=(anywhere(), anywhere(), vmem()),
        scratch_shapes=[
            pltpu.VMEM((10, EXT, LANES), jnp.float32),
            pltpu.VMEM((ROWS, LANES), jnp.int32),
            rim, rim, block, block,
            pltpu.VMEM((ny, 1, LANES), jnp.float32),
            pltpu.VMEM((nx, 1, LANES), jnp.float32),
            pltpu.SemaphoreType.DMA((4,)),
            pltpu.SemaphoreType.DMA((8,)),
            pltpu.SemaphoreType.DMA((8,)),
            pltpu.SemaphoreType.DMA((2,)),
            pltpu.SemaphoreType.DMA((2,)),
            pltpu.SemaphoreType.DMA((2,)),
        ]
        + view_scratch(),
        compiler_params=pltpu.CompilerParams(collective_id=0, has_side_effects=True, vmem_limit_bytes=LIMIT),
        name="flood",
    )(manning, depth_start, bed_height, zone_map, observe)
    return pl.pallas_call(
        finish_kernel,
        out_shape=(f32(EVENTS, ROWS, LANES), f32(EVENTS, ROWS, LANES), f32(ZONES)),
        in_specs=[vmem(), vmem(), vmem()],
        out_specs=(vmem(), vmem(), vmem()),
        compiler_params=pltpu.CompilerParams(vmem_limit_bytes=LIMIT),
        name="finish",
    )(final_windows, grad_windows, total)


def solution(mesh):
    in_specs = (P(None, "gy", "gx"), P("gy", "gx"), P("gy", "gx"), P(), P(None, "gy", "gx"))
    out_specs = (P(None, "gy", "gx"), P(None, "gy", "gx"), P())
    return jax.shard_map(body, mesh=mesh, in_specs=in_specs, out_specs=out_specs, check_vma=False)
```

time: 60 us -> 36.7 us (0.61)
  Pallas kernels: 57.9 us -> 35.9 us
  other arithmetic: 1.2 us -> 0 us
    pallas_call x3 -> x2, Pallas kernels: 57.9 us -> 35.9 us  [the longest x1 33.7 us: body(): pl.pallas_call(kernel, out_shape=(f32(WIDE, ROWS, LANES), f32(WIDE, ROWS,...]
    div x1 -> x0, other arithmetic: 1.2 us -> none  [body(): zone_grad = total[0, :ZONES] * (-2.0 / ALPHA) / manning]
where the time goes in v1:
time: 36.7 us; the launch traced here: 36.5 us
  Pallas kernels  35.9 us (98%)
  between operations  0.64 us (2%)
    pallas_call x1, Pallas kernels, body(): pl.pallas_call(kernel, out_shape=(f32(WIDE, ROWS, LANES), f32(WIDE, ROWS,...  33.7 us
    pallas_call x1, Pallas kernels, body(): pl.pallas_call(finish_kernel, out_shape=(f32(EVENTS, ROWS, LANES), f32(EV...  2.17 us

profile of v1, /device:TPU:1, one launch (start us, length us, event | category | flops | bytes accessed | tf_op | source)
XLA Modules:
  0.0 36.5 jit_solution(6171483452688801610)
XLA Ops:
  0.6 33.7 %flood.1 = (f32[5,128,128]{2,1,0:T(8,128)}, f32[5,128,128]{2,1,0:T(8,128)}, f32[1,128]{1,0:T(1,128)}) custom-call(f32[16]{0:T(128)} %manning.1, f32[4,128,128]{2,1,0:T(8,128)} %depth.1, f32[128,128]{1,0:T(8,128)} %bed.1, s32[128,128]{1,0:T(8,128)} %zone.1, f32[4,128,128]{2,1,0:T(8,128)} %observe.1), custom_call_target="tpu_custom_call" | custom-call | tf_op jit(solution)/shard_map/flood/pallas_call | solution.py:516
  34.4 2.2 %finish.1 = (f32[4,128,128]{2,1,0:T(8,128)}, f32[4,128,128]{2,1,0:T(8,128)}, f32[16]{0:T(128)}) custom-call(f32[5,128,128]{2,1,0:T(8,128)} %get-tuple-element.6.final_windows, f32[5,128,128]{2,1,0:T(8,128)} %get-tuple-element.7.grad_windows, f32[1,128]{1,0:T(1,128)} %get-tuple-element.8.total), custom_call_target="tpu_custom_call" | custom-call | tf_op jit(solution)/shard_map/finish/pallas_call | solution.py:538

commit v2 on v1

--- a/solution.py
+++ b/solution.py
@@ -81,12 +81,12 @@
 
 def pack_rims(ext, msg_left, msg_right):
     def one(i, carry):
-        here, own = pl.ds(pl.multiple_of(32 * i, 8), 32), pl.ds(pl.multiple_of(32 * i + RIM, 8), 32)
-        slot8 = lanes_of((32, LANES)) // 8
-        left = jnp.zeros((32, LANES), jnp.float32)
-        right = jnp.zeros((32, LANES), jnp.float32)
+        here, own = pl.ds(pl.multiple_of(64 * i, 8), 64), pl.ds(pl.multiple_of(64 * i + RIM, 8), 64)
+        slot8 = lanes_of((64, LANES)) // 8
+        left = jnp.zeros((64, LANES), jnp.float32)
+        right = jnp.zeros((64, LANES), jnp.float32)
         for q in range(10):
-            value = ext[q, own, :]
+            value = scaled(q, ext[q, own, :])
             right = jnp.where(slot8 == q, roll(value, 8 * q + 8), right)
             for e in range(EVENTS):
                 at = {e: 4 * e + 3, EVENTS + e: 4 * e + 2, 8: 4 * e + 1, 9: 4 * e}.get(q)
@@ -96,7 +96,7 @@
         msg_right[here, :] = right
         return carry
 
-    lax.fori_loop(0, ROWS // 32, one, 0)
+    lax.fori_loop(0, ROWS // 64, one, 0)
 
 
 def neighbours():
@@ -109,14 +109,14 @@
 def rim_copies(ext, col_left, col_right, msg_left, msg_right, send, recv):
     gy, gx, up, down, west, east = neighbours()
     plans = [
+        (msg_left.at[pl.ds(ROWS - RIM, RIM)], col_right.at[pl.ds(0, RIM)], (down, west)),
+        (msg_left.at[pl.ds(0, RIM)], col_right.at[pl.ds(RIM + ROWS, RIM)], (up, west)),
+        (msg_right.at[pl.ds(ROWS - RIM, RIM)], col_left.at[pl.ds(0, RIM)], (down, east)),
+        (msg_right.at[pl.ds(0, RIM)], col_left.at[pl.ds(RIM + ROWS, RIM)], (up, east)),
         (msg_left, col_right.at[pl.ds(RIM, ROWS)], (gy, west)),
         (msg_right, col_left.at[pl.ds(RIM, ROWS)], (gy, east)),
         (ext.at[:, pl.ds(ROWS, RIM)], ext.at[:, pl.ds(0, RIM)], (down, gx)),
         (ext.at[:, pl.ds(RIM, RIM)], ext.at[:, pl.ds(RIM + ROWS, RIM)], (up, gx)),
-        (msg_left.at[pl.ds(ROWS - RIM, RIM)], col_right.at[pl.ds(0, RIM)], (down, west)),
-        (msg_left.at[pl.ds(0, RIM)], col_right.at[pl.ds(RIM + ROWS, RIM)], (up, west)),
-        (msg_right.at[pl.ds(ROWS - RIM, RIM)], col_left.at[pl.ds(0, RIM)], (down, east)),
-        (msg_right.at[pl.ds(0, RIM)], col_left.at[pl.ds(RIM + ROWS, RIM)], (up, east)),
     ]
     return [
         pltpu.make_async_remote_copy(
@@ -134,63 +134,96 @@
 def greet_neighbours(barrier):
     gy, gx, up, down, west, east = neighbours()
     for to in [
+        (down, west),
+        (up, west),
+        (down, east),
+        (up, east),
         (gy, west),
         (gy, east),
         (down, gx),
         (up, gx),
-        (down, west),
-        (up, west),
-        (down, east),
-        (up, east),
     ]:
         pl.semaphore_signal(barrier, inc=1, device_id=to, device_id_type=MESH)
 
 
-def window_main(own, left, at):
-    lane = lanes_of(own.shape)
-    return jnp.where(lane < RIM, roll(left, -8 * at), roll(own, RIM))
-
-
-def window_side(owns, right, at):
+def scaled(q, value):
+    return value * ALPHA if q < EVENTS or q == 8 else value
+
+
+def window_side(owns):
     lane = lanes_of(owns[0].shape)
-    rolled = {}
-    out = roll(right, 24 - 8 * at)
-    for e, own in enumerate(owns):
-        hit = (lane >= 32 * e) & (lane < 32 * e + 24)
-        out = jnp.where(hit, roll(own, 24 + 32 * e), out)
+    out = roll(owns[0], 24)
+    for e in range(1, EVENTS):
+        out = jnp.where(lane >= 32 * e, roll(owns[e], 24 + 32 * e), out)
     return out
 
 
-def windows_chunk(r0, n, ext, col_left, col_right, depth, bar, gbx, gby, rough_x, rough_y, ground):
+def own_windows(ext, at):
+    value = [scaled(q, ext[q, at, :]) for q in range(10)]
+    mains = [roll(x, RIM) for x in value]
+    sides = [window_side(x) for x in (value[:EVENTS], value[EVENTS:8], [value[8]] * EVENTS, [value[9]] * EVENTS)]
+    return mains + sides
+
+
+def window_refs(v):
+    first, last = v.depth.at[0], v.bar.at[STEPS]
+    mains = [first.at[e] for e in range(EVENTS)] + [last.at[e] for e in range(EVENTS)]
+    mains += [v.ground.at[0], v.rough_x.at[0]]
+    return mains + [first.at[EVENTS], last.at[EVENTS], v.ground.at[1], v.rough_x.at[1]]
+
+
+def windows_before(ext, v):
+    def one(i, carry):
+        r0 = pl.multiple_of(32 * i, 8)
+        for ref, value in zip(window_refs(v), own_windows(ext, pl.ds(r0 + RIM, 32))):
+            ref[pl.ds(r0 + BASE + RIM, 32), :] = value
+        return carry
+
+    lax.fori_loop(0, ROWS // 32, one, 0)
+
+
+def windows_chunk(r0, n, ext, col_left, col_right, v, own):
     gy, gx, ny, nx = mesh_place()
     here, at = pl.ds(r0, n), pl.ds(r0 - BASE, n)
     left, right = col_left[at, :], col_right[at, :]
-    value = [ext[q, at, :] for q in range(10)]
-    for e in range(EVENTS):
-        depth[e, here, :] = window_main(value[e], left, e) * ALPHA
-        bar[e, here, :] = window_main(value[EVENTS + e], left, EVENTS + e)
-    depth[EVENTS, here, :] = window_side(value[:EVENTS], right, 3) * ALPHA
-    bar[EVENTS, here, :] = window_side(value[EVENTS:8], right, 2)
-    shape = (n, LANES)
-    lane = lanes_of(shape)
-    row = rows_of(shape) + (gy * ROWS - RIM - BASE + r0)
+    refs = window_refs(v)
+    values = [ref[here, :] for ref in refs] if own else own_windows(ext, at)
+    lane = lanes_of((n, LANES))
+    for q in range(10):
+        values[q] = jnp.where(lane < RIM, roll(left, -8 * q), values[q])
+    tail = lane % 32 >= 24
+    for i in range(4):
+        values[10 + i] = jnp.where(tail, roll(right, 8 * i), values[10 + i])
+    row = rows_of((n, LANES)) + (gy * ROWS - RIM - BASE + r0)
     wall_y = (row < 0) | (row >= ny * ROWS - 1)
+    for ref, value in zip(refs[:9] + refs[10:13], values[:9] + values[10:13]):
+        ref[here, :] = value
     for w in range(2):
-        if w == 0:
-            high = window_main(value[8], left, 8)
-            rough = window_main(value[9], left, 9)
-            column = lane + (gx * LANES - RIM)
-        else:
-            high = window_side([value[8]] * EVENTS, right, 1)
-            rough = window_side([value[9]] * EVENTS, right, 0)
-            column = lane % 32 + (gx * LANES + 104)
-        high = high * ALPHA
-        ground[w, here, :] = high
-        gbx[w, here, :] = roll(high, -1) - high
-        gby[w, pl.ds(r0 - 8, n), :] = ground[w, pl.ds(r0 - 7, n), :] - ground[w, pl.ds(r0 - 8, n), :]
+        ground, rough = (values[8], values[9]) if w == 0 else (values[12], values[13])
+        column = lane + (gx * LANES - RIM) if w == 0 else lane % 32 + (gx * LANES + 104)
         wall_x = (column < 0) | (column >= nx * LANES - 1)
-        rough_x[w, here, :] = jnp.where(wall_x, WALL, rough)
-        rough_y[w, here, :] = jnp.where(wall_y, WALL, rough)
+        v.gbx[w, here, :] = roll(ground, -1) - ground
+        v.rough_x[w, here, :] = jnp.where(wall_x, WALL, rough)
+        v.rough_y[w, here, :] = jnp.where(wall_y, WALL, rough)
+        if own:
+            fall(v, w, r0 - 8, n)
+
+
+def fall(v, w, r0, n):
+    v.gby[w, pl.ds(r0, n), :] = v.ground[w, pl.ds(r0 + 1, n), :] - v.ground[w, pl.ds(r0, n), :]
+
+
+def windows_after(ext, col_left, col_right, v):
+    windows_chunk(BASE, RIM, ext, col_left, col_right, v, False)
+
+    def one(i, carry):
+        windows_chunk(pl.multiple_of(32 * i, 8) + BASE + RIM, 32, ext, col_left, col_right, v, True)
+        return carry
+
+    lax.fori_loop(0, ROWS // 32, one, 0)
+    windows_chunk(BASE + RIM + ROWS, RIM, ext, col_left, col_right, v, False)
+    for w in range(2):
+        fall(v, w, BASE + EXT - 16, 16)
 
 
 def inverse(x):
@@ -206,15 +239,17 @@
         drag = drag * (BETA * FLOOR)
         keep = inverse(drag + 1.0 / SIDE)
         new = keep * (-drive)
+        term = new * drag
+        own = None
     else:
         size = flux * flux + FLOOR_SQ
-        turn = lax.rsqrt(size)
-        drag = drag * (size * turn)
-        keep = inverse(drag + 1.0 / SIDE)
+        drag = drag * lax.rsqrt(size)
+        keep = inverse(drag * size + 1.0 / SIDE)
         new = keep * ((MID * flux + sides) - drive)
-    term = new * drag
+        drag = new * drag
+        term = drag * size
+        own = MID - drag * flux
     both = ((-POWER) * term) * inverse(double) - slope
-    own = None if first else MID - term * ((flux * turn) * turn)
     return new, keep, term, both + double, both - double, own
 
 
@@ -254,10 +289,11 @@
     for k in range(WIDE):
         w = k // EVENTS
         bar_d = v.bar[t + 1, k, here, :]
-        back_x = roll(bar_d, -1) - bar_d
         back_y = v.bar[t + 1, k, below, :] - bar_d
-        if not last:
-            back_x = back_x + v.bar_x[t + 1, k, here, :]
+        if last:
+            back_x = roll(bar_d, -1) - bar_d
+        else:
+            back_x = v.back_x[t + 1, k, here, :]
             back_y = back_y + (
                 v.bar_y[t + 1, k, here, :] + (v.side_y[t + 1, k, above, :] + v.side_y[t + 1, k, below, :])
             )
@@ -270,12 +306,12 @@
             v.side_x[k, here, :] = ax
             continue
         v.down_y[k, here, :] = ay * v.next_y[t, k, here, :]
-        v.bar[t, k, here, :] = (
-            bar_d
-            + (ax * v.here_x[t, k, here, :] + roll(ax * v.next_x[t, k, here, :], 1))
-            + (ay * v.here_y[t, k, here, :] + v.down_y[k, above, :])
+        base = (bar_d + ax * v.here_x[t, k, here, :]) + (ay * v.here_y[t, k, here, :] + v.down_y[k, above, :])
+        right = ax * v.next_x[t, k, here, :]
+        v.bar[t, k, here, :] = base + roll(right, 1)
+        v.back_x[t, k, here, :] = (roll(base + ax, -1) + roll(ax - right, 1)) + (
+            (right + ax * v.own_x[t, k, here, :]) - base
         )
-        v.bar_x[t, k, here, :] = ax * v.own_x[t, k, here, :] + (roll(ax, 1) + roll(ax, -1))
         v.bar_y[t, k, here, :] = ay * v.own_y[t, k, here, :]
     for w in range(2):
         if last:
@@ -296,8 +332,18 @@
         )
 
 
-def unwindow(window, side, e):
-    return jnp.where(lanes_of(side.shape) < 112, roll(window, -RIM), roll(side, 104 - 32 * e))
+def unwindow(source, target, scale):
+    def one(i, carry):
+        at = pl.ds(pl.multiple_of(64 * i, 8), 64)
+        here = pl.ds(pl.multiple_of(64 * i, 8) + BASE + RIM, 64)
+        side = source[EVENTS, here, :]
+        lane = lanes_of(side.shape)
+        for e in range(EVENTS):
+            own = jnp.where(lane < 112, roll(source[e, here, :], -RIM), roll(side, 104 - 32 * e))
+            target[e, at, :] = own if scale is None else own * scale
+        return carry
+
+    lax.fori_loop(0, ROWS // 64, one, 0)
 
 
 def class_row(manning, zone, classes):
@@ -336,13 +382,13 @@
 
 
 CHUNK_F = 72
-CHUNK_B = 72
+CHUNK_B = 144
 CHUNK_W = 48
 CHUNK_A = 72
 
 
 FULL = ("fx", "fy", "keep_x", "keep_y", "term_x", "term_y", "here_x", "here_y", "next_x", "next_y", "own_x", "own_y")
-FULL += ("bar_x", "bar_y", "side_y")
+FULL += ("back_x", "bar_y", "side_y")
 PLANE = ("ground", "gbx", "gby", "rough_x", "rough_y", "classes")
 NAMES = FULL + PLANE + ("depth", "bar", "side_x", "down_y")
 Views = collections.namedtuple("Views", NAMES)
@@ -371,12 +417,7 @@
 LOOP_T = False
 
 
-def forward(v, ext, col_left, col_right):
-    chunks(CHUNK_W, lambda r0, n: windows_chunk(
-        r0, n, ext, col_left, col_right, v.depth.at[0], v.bar.at[STEPS], v.gbx, v.gby, v.rough_x, v.rough_y, v.ground))
-    last = pl.ds(BASE + EXT - 8, 8)
-    for w in range(2):
-        v.gby[w, last, :] = v.ground[w, pl.ds(BASE + EXT - 7, 8), :] - v.ground[w, last, :]
+def forward(v):
     chunks(CHUNK_F, lambda r0, n: forward_chunk(True, False, 0, r0, n, v))
     over_steps(1, STEPS, False, lambda t: chunks(CHUNK_F, lambda r0, n: forward_chunk(False, False, t, r0, n, v)))
 
@@ -443,16 +484,16 @@
 
 def kernel(
     manning, depth, bed, zone, observe, final, grad, total,
-    ext, zone_here, col_left, col_right, msg_left, msg_right, slots_y, slots_x,
+    ext, zone_here, col_left, col_right, msg_left, msg_right, final_here, grad_here, slots_y, slots_x,
     own_sems, rim_send, rim_recv, sum_send, sum_recv, out_sems, *views,
 ):
     v = Views(*views)
     gy, gx, ny, nx = mesh_place()
     barrier = pltpu.get_barrier_semaphore()
     copies = own_copies(depth, bed, zone, observe, ext, zone_here, own_sems)
+    greet_neighbours(barrier)
     for copy in copies:
         copy.start()
-    greet_neighbours(barrier)
     greet_stage(barrier, 0)
     greet_stage(barrier, 1)
     for copy in copies:
@@ -463,23 +504,26 @@
     rims = rim_copies(ext, col_left, col_right, msg_left, msg_right, rim_send, rim_recv)
     for copy in rims:
         copy.start()
+    windows_before(ext, v)
     for copy in rims:
         copy.wait()
-    forward(v, ext, col_left, col_right)
-    own = pl.ds(BASE + RIM, ROWS)
-    final_copy = pltpu.make_async_copy(v.depth.at[STEPS, :, own], final, out_sems.at[0])
-    final_copy.start()
+    windows_after(ext, col_left, col_right, v)
+    forward(v)
     backward(v)
     send_stage(0, class_row(manning, zone_here, v.classes), slots_y, sum_send, sum_recv)
     chunks(CHUNK_A, lambda r0, n: start_chunk(r0, n, v))
-    grad_copy = pltpu.make_async_copy(v.bar.at[0, :, own], grad, out_sems.at[1])
+    unwindow(v.bar.at[0], grad_here, None)
+    grad_copy = pltpu.make_async_copy(grad_here, grad, out_sems.at[0])
     grad_copy.start()
+    unwindow(v.depth.at[STEPS], final_here, 1.0 / ALPHA)
+    final_copy = pltpu.make_async_copy(final_here, final, out_sems.at[1])
+    final_copy.start()
     send_stage(1, sum_stage(0, slots_y, sum_recv), slots_x, sum_send, sum_recv)
+    grad_copy.wait()
     final_copy.wait()
     drain_stage(0, slots_y, sum_send)
-    total[...] = sum_stage(1, slots_x, sum_recv)
+    total[...] = sum_stage(1, slots_x, sum_recv)[0, :ZONES]
     drain_stage(1, slots_x, sum_send)
-    grad_copy.wait()
 
 
 def vmem():
@@ -497,12 +541,10 @@
 LIMIT = 60 * 1024 * 1024
 
 
-def finish_kernel(final_windows, grad_windows, total, final, grad, zone_grad):
-    final_side, grad_side = final_windows[EVENTS], grad_windows[EVENTS]
-    for e in range(EVENTS):
-        final[e] = unwindow(final_windows[e], final_side, e) * (1.0 / ALPHA)
-        grad[e] = unwindow(grad_windows[e], grad_side, e)
-    zone_grad[...] = total[0, :ZONES]
+def finish_kernel(final_here, grad_here, sums_here, final, grad, sums):
+    final[...] = final_here[...]
+    grad[...] = grad_here[...]
+    sums[...] = sums_here[...]
 
 
 def anywhere():
@@ -512,16 +554,17 @@
 def body(depth_start, bed_height, zone_map, manning, observe):
     ny, nx = lax.axis_size("gy"), lax.axis_size("gx")
     block = pltpu.VMEM((ROWS, LANES), jnp.float32)
+    blocks = pltpu.VMEM((EVENTS, ROWS, LANES), jnp.float32)
     rim = pltpu.VMEM((EXT, LANES), jnp.float32)
-    final_windows, grad_windows, total = pl.pallas_call(
+    final, grad, sums = pl.pallas_call(
         kernel,
-        out_shape=(f32(WIDE, ROWS, LANES), f32(WIDE, ROWS, LANES), f32(1, LANES)),
+        out_shape=(f32(EVENTS, ROWS, LANES), f32(EVENTS, ROWS, LANES), f32(ZONES)),
         in_specs=[smem(), anywhere(), anywhere(), anywhere(), anywhere()],
         out_specs=(anywhere(), anywhere(), vmem()),
         scratch_shapes=[
             pltpu.VMEM((10, EXT, LANES), jnp.float32),
             pltpu.VMEM((ROWS, LANES), jnp.int32),
-            rim, rim, block, block,
+            rim, rim, block, block, blocks, blocks,
             pltpu.VMEM((ny, 1, LANES), jnp.float32),
             pltpu.VMEM((nx, 1, LANES), jnp.float32),
             pltpu.SemaphoreType.DMA((4,)),
@@ -542,7 +585,7 @@
         out_specs=(vmem(), vmem(), vmem()),
         compiler_params=pltpu.CompilerParams(vmem_limit_bytes=LIMIT),
         name="finish",
-    )(final_windows, grad_windows, total)
+    )(final, grad, sums)
 
 
 def solution(mesh):

time: 36.7 us -> 34.8 us (0.948)
  Pallas kernels: 35.9 us -> 34 us
    pallas_call x1, Pallas kernels: 33.7 us -> 32.1 us  [body(): pl.pallas_call(kernel, out_shape=(f32(EVENTS, ROWS, LANES), f32(EVENTS, R...]
where the time goes in v2:
time: 34.8 us; the launch traced here: 34.6 us
  Pallas kernels  34 us (98%)
  between operations  0.64 us (2%)
    pallas_call x1, Pallas kernels, body(): pl.pallas_call(kernel, out_shape=(f32(EVENTS, ROWS, LANES), f32(EVENTS, R...  32.1 us
    pallas_call x1, Pallas kernels, body(): pl.pallas_call(finish_kernel, out_shape=(f32(EVENTS, ROWS, LANES), f32(EV...  1.84 us

profile of v2, /device:TPU:1, one launch (start us, length us, event | category | flops | bytes accessed | tf_op | source)
XLA Modules:
  0.0 34.6 jit_solution(9481423770922287361)
XLA Ops:
  0.6 32.1 %flood.1 = (f32[4,128,128]{2,1,0:T(8,128)}, f32[4,128,128]{2,1,0:T(8,128)}, f32[16]{0:T(128)}) custom-call(f32[16]{0:T(128)} %manning.1, f32[4,128,128]{2,1,0:T(8,128)} %depth.1, f32[128,128]{1,0:T(8,128)} %bed.1, s32[128,128]{1,0:T(8,128)} %zone.1, f32[4,128,128]{2,1,0:T(8,128)} %observe.1), custom_call_target="tpu_custom_call" | custom-call | tf_op jit(solution)/shard_map/flood/pallas_call | solution.py:559
  32.8 1.8 %finish.1 = (f32[4,128,128]{2,1,0:T(8,128)}, f32[4,128,128]{2,1,0:T(8,128)}, f32[16]{0:T(128)}) custom-call(f32[4,128,128]{2,1,0:T(8,128)} %get-tuple-element.6.final_here, f32[4,128,128]{2,1,0:T(8,128)} %get-tuple-element.7.grad_here, f32[16]{0:T(128)} %get-tuple-element.8.sums_here), custom_call_target="tpu_custom_call" | custom-call | tf_op jit(solution)/shard_map/finish/pallas_call | solution.py:581

commit v3 on v2

--- a/solution.py
+++ b/solution.py
@@ -81,10 +81,10 @@
 
 def pack_rims(ext, msg_left, msg_right):
     def one(i, carry):
-        here, own = pl.ds(pl.multiple_of(64 * i, 8), 64), pl.ds(pl.multiple_of(64 * i + RIM, 8), 64)
-        slot8 = lanes_of((64, LANES)) // 8
-        left = jnp.zeros((64, LANES), jnp.float32)
-        right = jnp.zeros((64, LANES), jnp.float32)
+        here, own = pl.ds(pl.multiple_of(128 * i, 8), 128), pl.ds(pl.multiple_of(128 * i + RIM, 8), 128)
+        slot8 = lanes_of((128, LANES)) // 8
+        left = jnp.zeros((128, LANES), jnp.float32)
+        right = jnp.zeros((128, LANES), jnp.float32)
         for q in range(10):
             value = scaled(q, ext[q, own, :])
             right = jnp.where(slot8 == q, roll(value, 8 * q + 8), right)
@@ -96,7 +96,7 @@
         msg_right[here, :] = right
         return carry
 
-    lax.fori_loop(0, ROWS // 64, one, 0)
+    lax.fori_loop(0, ROWS // 128, one, 0)
 
 
 def neighbours():
@@ -174,12 +174,12 @@
 
 def windows_before(ext, v):
     def one(i, carry):
-        r0 = pl.multiple_of(32 * i, 8)
-        for ref, value in zip(window_refs(v), own_windows(ext, pl.ds(r0 + RIM, 32))):
-            ref[pl.ds(r0 + BASE + RIM, 32), :] = value
+        r0 = pl.multiple_of(128 * i, 8)
+        for ref, value in zip(window_refs(v), own_windows(ext, pl.ds(r0 + RIM, 128))):
+            ref[pl.ds(r0 + BASE + RIM, 128), :] = value
         return carry
 
-    lax.fori_loop(0, ROWS // 32, one, 0)
+    lax.fori_loop(0, ROWS // 128, one, 0)
 
 
 def windows_chunk(r0, n, ext, col_left, col_right, v, own):
@@ -216,11 +216,7 @@
 def windows_after(ext, col_left, col_right, v):
     windows_chunk(BASE, RIM, ext, col_left, col_right, v, False)
 
-    def one(i, carry):
-        windows_chunk(pl.multiple_of(32 * i, 8) + BASE + RIM, 32, ext, col_left, col_right, v, True)
-        return carry
-
-    lax.fori_loop(0, ROWS // 32, one, 0)
+    windows_chunk(BASE + RIM, ROWS, ext, col_left, col_right, v, True)
     windows_chunk(BASE + RIM + ROWS, RIM, ext, col_left, col_right, v, False)
     for w in range(2):
         fall(v, w, BASE + EXT - 16, 16)
@@ -234,7 +230,7 @@
     double = depth + depth_next
     slope = (depth_next - depth) + gap
     drive = double * slope
-    drag = rough * jnp.exp2((POWER / 0.6931471805599453) * jnp.log(double))
+    drag = rough * jnp.exp2(POWER * jnp.log2(double))
     if first:
         drag = drag * (BETA * FLOOR)
         keep = inverse(drag + 1.0 / SIDE)
@@ -381,7 +377,7 @@
     lax.fori_loop(0, EXT // rows, one, 0)
 
 
-CHUNK_F = 72
+CHUNK_F = 144
 CHUNK_B = 144
 CHUNK_W = 48
 CHUNK_A = 72

time: 34.8 us -> 34 us (0.977)
  Pallas kernels: 34 us -> 33.2 us
    pallas_call x1, Pallas kernels: 32.1 us -> 31.3 us  [body(): pl.pallas_call(kernel, out_shape=(f32(EVENTS, ROWS, LANES), f32(EVENTS, R...]
where the time goes in v3:
time: 34 us; the launch traced here: 33.8 us
  Pallas kernels  33.2 us (98%)
  between operations  0.64 us (2%)
    pallas_call x1, Pallas kernels, body(): pl.pallas_call(kernel, out_shape=(f32(EVENTS, ROWS, LANES), f32(EVENTS, R...  31.3 us
    pallas_call x1, Pallas kernels, body(): pl.pallas_call(finish_kernel, out_shape=(f32(EVENTS, ROWS, LANES), f32(EV...  1.84 us

profile of v3, /device:TPU:1, one launch (start us, length us, event | category | flops | bytes accessed | tf_op | source)
XLA Modules:
  0.0 33.8 jit_solution(15093858560597993476)
XLA Ops:
  0.6 31.3 %flood.1 = (f32[4,128,128]{2,1,0:T(8,128)}, f32[4,128,128]{2,1,0:T(8,128)}, f32[16]{0:T(128)}) custom-call(f32[16]{0:T(128)} %manning.1, f32[4,128,128]{2,1,0:T(8,128)} %depth.1, f32[128,128]{1,0:T(8,128)} %bed.1, s32[128,128]{1,0:T(8,128)} %zone.1, f32[4,128,128]{2,1,0:T(8,128)} %observe.1), custom_call_target="tpu_custom_call" | custom-call | tf_op jit(solution)/shard_map/flood/pallas_call | solution.py:555
  32.0 1.8 %finish.1 = (f32[4,128,128]{2,1,0:T(8,128)}, f32[4,128,128]{2,1,0:T(8,128)}, f32[16]{0:T(128)}) custom-call(f32[4,128,128]{2,1,0:T(8,128)} %get-tuple-element.6.final_here, f32[4,128,128]{2,1,0:T(8,128)} %get-tuple-element.7.grad_here, f32[16]{0:T(128)} %get-tuple-element.8.sums_here), custom_call_target="tpu_custom_call" | custom-call | tf_op jit(solution)/shard_map/finish/pallas_call | solution.py:577

commit v4 on v3

--- a/solution.py
+++ b/solution.py
@@ -206,7 +206,7 @@
         v.rough_x[w, here, :] = jnp.where(wall_x, WALL, rough)
         v.rough_y[w, here, :] = jnp.where(wall_y, WALL, rough)
         if own:
-            fall(v, w, r0 - 8, n)
+            fall(v, w, r0, n - 8)
 
 
 def fall(v, w, r0, n):
@@ -215,10 +215,9 @@
 
 def windows_after(ext, col_left, col_right, v):
     windows_chunk(BASE, RIM, ext, col_left, col_right, v, False)
-
-    windows_chunk(BASE + RIM, ROWS, ext, col_left, col_right, v, True)
     windows_chunk(BASE + RIM + ROWS, RIM, ext, col_left, col_right, v, False)
     for w in range(2):
+        fall(v, w, BASE, RIM)
         fall(v, w, BASE + EXT - 16, 16)
 
 
@@ -501,7 +500,10 @@
     for copy in rims:
         copy.start()
     windows_before(ext, v)
-    for copy in rims:
+    for copy in rims[4:6]:
+        copy.wait()
+    windows_chunk(BASE + RIM, ROWS, ext, col_left, col_right, v, True)
+    for copy in rims[:4] + rims[6:]:
         copy.wait()
     windows_after(ext, col_left, col_right, v)
     forward(v)

time: 34 us -> 33.5 us (0.985)
  Pallas kernels: 33.2 us -> 32.7 us
    pallas_call x1, Pallas kernels: 31.3 us -> 30.9 us  [body(): pl.pallas_call(kernel, out_shape=(f32(EVENTS, ROWS, LANES), f32(EVENTS, R...]
where the time goes in v4:
time: 33.5 us; the launch traced here: 33.4 us
  Pallas kernels  32.7 us (98%)
  between operations  0.64 us (2%)
    pallas_call x1, Pallas kernels, body(): pl.pallas_call(kernel, out_shape=(f32(EVENTS, ROWS, LANES), f32(EVENTS, R...  30.9 us
    pallas_call x1, Pallas kernels, body(): pl.pallas_call(finish_kernel, out_shape=(f32(EVENTS, ROWS, LANES), f32(EV...  1.84 us

profile of v4, /device:TPU:1, one launch (start us, length us, event | category | flops | bytes accessed | tf_op | source)
XLA Modules:
  0.0 33.4 jit_solution(5934978645559896334)
XLA Ops:
  0.6 30.9 %flood.1 = (f32[4,128,128]{2,1,0:T(8,128)}, f32[4,128,128]{2,1,0:T(8,128)}, f32[16]{0:T(128)}) custom-call(f32[16]{0:T(128)} %manning.1, f32[4,128,128]{2,1,0:T(8,128)} %depth.1, f32[128,128]{1,0:T(8,128)} %bed.1, s32[128,128]{1,0:T(8,128)} %zone.1, f32[4,128,128]{2,1,0:T(8,128)} %observe.1), custom_call_target="tpu_custom_call" | custom-call | tf_op jit(solution)/shard_map/flood/pallas_call | solution.py:557
  31.5 1.8 %finish.1 = (f32[4,128,128]{2,1,0:T(8,128)}, f32[4,128,128]{2,1,0:T(8,128)}, f32[16]{0:T(128)}) custom-call(f32[4,128,128]{2,1,0:T(8,128)} %get-tuple-element.6.final_here, f32[4,128,128]{2,1,0:T(8,128)} %get-tuple-element.7.grad_here, f32[16]{0:T(128)} %get-tuple-element.8.sums_here), custom_call_target="tpu_custom_call" | custom-call | tf_op jit(solution)/shard_map/finish/pallas_call | solution.py:579
